TPU v7x, 1024 devices: a whole 8x8x8 slice. The times are simulated.
1024 devices in a mesh: gx: 4 (over z_lo), gy: 16 (over z_hi, y), gz: 16 (over x, core).
Axes of the slice: x: 8, y: 8, z: 8 (z_hi: 2, z_lo: 4; z = z_hi * 4 + z_lo), core: 2. Of those that a mesh axis runs over, the one named last changes fastest.
Arguments:
- solution: float32 [56, 9, 131072], P(None, None, ('gx', 'gy', 'gz')), may hold values from -6 to 6
- jacobians: float32 [3, 9, 9, 131072], P(None, None, None, ('gx', 'gy', 'gz')), may hold values from -2 to 2
- derivative_stiffness: float32 [3, 56, 56], replicated, may hold values from -0.75 to 0.75
- volume_stiffness: float32 [3, 56, 56], replicated, may hold values from -0.375 to 0.375
- face_project: float32 [4, 21, 56], replicated, may hold values from -0.75 to 0.75
- face_lift: float32 [4, 56, 21], replicated, may hold values from -0.625 to 0.625
- face_rotation: float32 [3, 21, 21], replicated, may hold values from -1.25 to 1.25
- local_solver: float32 [4, 9, 9, 131072], P(None, None, None, ('gx', 'gy', 'gz')), may hold values from -2 to 2
- neighbour_solver: float32 [4, 9, 9, 131072], P(None, None, None, ('gx', 'gy', 'gz')), may hold values from -2 to 2
- cluster: int32 [131072], P(('gx', 'gy', 'gz')), may hold values from 0 to 2
- neighbours: int32 [4, 131072], P(None, ('gx', 'gy', 'gz')), may hold values from 0 to 1279, as said below
- orient: int32 [4, 131072], P(None, ('gx', 'gy', 'gz')), may hold values from 0 to 2
- send_faces: int32 [6, 131072], P(None, ('gx', 'gy', 'gz')), may hold values from 0 to 511
- counts: int32 [6, 1024], P(None, ('gx', 'gy', 'gz')), may hold values from 64 to 128, as said below
Outputs:
- advanced: float32 [56, 9, 131072], P(None, None, ('gx', 'gy', 'gz'))
Inputs may be any that keep to these rules, and one draw needn't show every extreme that they name: `neighbours`: below 512 a value names a face of the own partition; above, a slot of the blocks of one direction whose index is below the sending partition's count for that list. `send_faces`: each value is a local face j * 128 + n of the sending partition. `counts`: entry [k, p] is how many leading slots of partition p's list k are used; some entry equals 128.
All inputs are finite; a program needn't handle non-finite values.
Results may differ from a plain program's by a relative error of at most 0.0001.
Values sent between devices are 32-bit elements; how exact they have to be, the bound alone decides.
A program may use at most 64 MiB of HBM per device.

v0:
```python
import math

import jax
import jax.numpy as jnp
from jax import lax
from jax.sharding import PartitionSpec as P

BASIS = 56
QUANTITIES = 9
FACE_BASIS = 21
DERIVATIVES = 6
SUBSTEPS = 4


highest = lax.Precision.HIGHEST
coarse_span = 1.0


def shifted(value, axis, steps):
    count = lax.axis_size(axis)
    leading, last = (max(0, -steps), min(count, count - steps))
    return lax.ppermute(value, axis, [(source, source + steps) for source in range(leading, last)])


def small_apply(values, matrices):
    return jnp.sum(values[:, :, :, None, :] * matrices[:, None, :, :, :], axis=2)


def derivative_terms(solution, jacobians, stiff_stack):
    current = solution
    results = [solution]
    for power_index in range(DERIVATIVES - 1):
        mixed_terms = jnp.dot(stiff_stack, current.reshape(BASIS, -1), precision=highest).reshape(
            3, BASIS, QUANTITIES, -1
        )
        current = -jnp.sum(small_apply(mixed_terms, jacobians), axis=0)
        results.append(current)
    return results


def time_weights(cluster, substep):
    period = jnp.left_shift(jnp.ones_like(cluster), cluster)
    offset = (substep % period).astype(jnp.float32)
    finish = (substep + 1) % period == 0
    substep_span = coarse_span / SUBSTEPS
    upper_time = (offset + 1.0) * substep_span
    lower_time = offset * substep_span
    weight_rows = [
        (upper_time ** (power_index + 1) - lower_time ** (power_index + 1))
        / math.factorial(power_index + 1)
        for power_index in range(DERIVATIVES)
    ]
    return (jnp.stack(weight_rows), finish)


def volume_term(accumulated, jacobians, volume_stack):
    mixed_terms = jnp.dot(volume_stack, accumulated.reshape(BASIS, -1), precision=highest).reshape(
        3, BASIS, QUANTITIES, -1
    )
    return jnp.sum(small_apply(mixed_terms, jacobians), axis=0)


def trade(outgoing):
    pieces = []
    for which_side, shift_step in ((0, 1), (1, -1)):
        pieces.append(shifted(outgoing[which_side], "gx", shift_step))
    for which_side, shift_step in ((0, 1), (1, -1)):
        pieces.append(shifted(outgoing[2 + which_side], "gy", shift_step))
    for which_side, shift_step in ((0, 1), (1, -1)):
        pieces.append(shifted(outgoing[4 + which_side], "gz", shift_step))
    return jnp.concatenate(pieces, axis=1)


def local(
    solution,
    jacobians,
    derivative_stiffness,
    volume_stiffness,
    face_project,
    face_lift,
    face_rotation,
    local_solver,
    neighbour_solver,
    cluster,
    neighbours,
    orient,
    send_faces,
    counts,
):
    elements = solution.shape[2]
    face_count = 4 * elements
    slot_count = send_faces.shape[1]
    block_width = FACE_BASIS * QUANTITIES
    stiff_stack = derivative_stiffness.reshape(3 * BASIS, BASIS)
    volume_stack = volume_stiffness.reshape(3 * BASIS, BASIS)
    project_stack = face_project.reshape(4 * FACE_BASIS, BASIS)
    rotation_stack = face_rotation.reshape(3 * FACE_BASIS, FACE_BASIS)
    lift_faces = face_lift.transpose(1, 0, 2)
    live_slots = jnp.arange(slot_count, dtype=jnp.int32)[None, :] < counts
    orient_picks = (orient[None, :, :] == jnp.arange(3, dtype=jnp.int32)[:, None, None]).astype(
        jnp.float32
    )
    neighbour_flat = neighbours.reshape(-1)
    send_flat = send_faces.reshape(-1)
    local_turned = local_solver.transpose(1, 2, 0, 3)
    neighbour_turned = neighbour_solver.transpose(1, 2, 0, 3)
    own_total = jnp.zeros_like(solution)
    flux_total = jnp.zeros_like(solution)
    for substep in range(SUBSTEPS):
        weights, finish = time_weights(cluster, substep)
        derivatives = derivative_terms(solution, jacobians, stiff_stack)
        integral = weights[0][None, None, :] * derivatives[0]
        for power_index in range(1, DERIVATIVES):
            integral = integral + weights[power_index][None, None, :] * derivatives[power_index]
        projected = jnp.dot(project_stack, integral.reshape(BASIS, -1), precision=highest).reshape(
            4, FACE_BASIS, QUANTITIES, elements
        )
        own_table = (
            projected.reshape(4, block_width, elements)
            .transpose(1, 0, 2)
            .reshape(block_width, face_count)
        )
        outgoing = (
            jnp.take(own_table, send_flat, axis=1)
            .reshape(block_width, 6, slot_count)
            .transpose(1, 0, 2)
        )
        outgoing = jnp.where(live_slots[:, None, :], outgoing, 0.0)
        incoming = trade(outgoing)
        face_table = jnp.concatenate([own_table, incoming], axis=1)
        gathered = jnp.take(face_table, neighbour_flat, axis=1)
        rotated = jnp.dot(
            rotation_stack, gathered.reshape(FACE_BASIS, -1), precision=highest
        ).reshape(3, FACE_BASIS, QUANTITIES, 4, elements)
        chosen = jnp.sum(rotated * orient_picks[:, None, None, :, :], axis=0)
        neighbour_part = jnp.sum(chosen[:, :, None, :, :] * neighbour_turned[None], axis=1)
        face_local = projected.transpose(1, 2, 0, 3)
        local_part = jnp.sum(face_local[:, :, None, :, :] * local_turned[None], axis=1)
        flux_step = jnp.einsum(
            "kif,fpie->kpe", lift_faces, local_part + neighbour_part, precision=highest
        )
        own_total = own_total + integral
        flux_total = flux_total + flux_step
        updated = solution + volume_term(own_total, jacobians, volume_stack) - flux_total
        ending = finish[None, None, :]
        solution = jnp.where(ending, updated, solution)
        own_total = jnp.where(ending, 0.0, own_total)
        flux_total = jnp.where(ending, 0.0, flux_total)
    return solution


def solution(mesh):
    return jax.shard_map(
        local,
        mesh=mesh,
        in_specs=(
            P(None, None, ("gx", "gy", "gz")),
            P(None, None, None, ("gx", "gy", "gz")),
            P(),
            P(),
            P(),
            P(),
            P(),
            P(None, None, None, ("gx", "gy", "gz")),
            P(None, None, None, ("gx", "gy", "gz")),
            P(("gx", "gy", "gz")),
            P(None, ("gx", "gy", "gz")),
            P(None, ("gx", "gy", "gz")),
            P(None, ("gx", "gy", "gz")),
            P(None, ("gx", "gy", "gz")),
        ),
        out_specs=P(None, None, ("gx", "gy", "gz")),
        check_vma=False,
    )
```

profile of v0, /device:TPU:119, one launch (start us, length us, event | category | flops | bytes accessed | tf_op | source)
XLA Modules:
  0.0 254.0 jit_solution(12537836050415231573)
XLA Ops:
  2.4 1.8 fusion.61
  15.6 2.1 gather_fusion
  19.0 5.7 %collective-permute-start = (f32[189,128]{0,1:T(8,128)}, f32[189,128]{0,1:T(8,128)}, u32[]{:S(2)}, u32[]{:S(2)}) collective-permute-start(f32[189,128]{0,1:T(8,128)} %get-tuple-element.46), channel_id=1, source_target_pairs={{0,256},{256,512},{512,768},{1,257},{257,513},{513,769},{2,258},{2... | collective-permute-start | bytes 290312 | tf_op jit(solution)/shard_map/ppermute | solution.py:22
  26.0 11.8 %collective-permute-start.2 = (f32[189,128]{0,1:T(8,128)}, f32[189,128]{0,1:T(8,128)}, u32[]{:S(2)}, u32[]{:S(2)}) collective-permute-start(f32[189,128]{0,1:T(8,128)} %get-tuple-element.44), channel_id=1, source_target_pairs={{0,16},{16,32},{32,48},{48,64},{64,80},{80,96},{96,112},{112,128},... | collective-permute-start | bytes 290312 | tf_op jit(solution)/shard_map/ppermute | solution.py:22
  37.8 1.9 collective-permute-start.3
  39.7 5.7 %collective-permute-start.4 = (f32[189,128]{0,1:T(8,128)}, f32[189,128]{0,1:T(8,128)}, u32[]{:S(2)}, u32[]{:S(2)}) collective-permute-start(f32[189,128]{0,1:T(8,128)} %get-tuple-element.42), channel_id=1, source_target_pairs={{0,1},{1,2},{2,3},{3,4},{4,5},{5,6},{6,7},{7,8},{8,9},{9,10},{10,1... | collective-permute-start | bytes 290312 | tf_op jit(solution)/shard_map/ppermute | solution.py:22
  49.3 1.7 convolution_bitcast_fusion.22
  55.7 1.9 collective-permute-start.5
  63.2 1.6 gather_fusion.1
  80.4 13.4 %multiply_reduce_fusion.13 = f32[56,9,128]{2,0,1:T(8,128)S(1)} fusion(f32[3,56,9,128]{3,1,2,0:T(8,128)S(1)} %copy.106, f32[3,9,9,128]{3,2,1,0:T(8,128)S(1)} %copy.79), kind=kLoop, calls=%fused_computation.21 | loop fusion | flops 3419136 | bytes 1156608 | tf_op jit(solution)/shard_map/reduce_sum | solution.py:36
  100.9 2.1 gather_fusion.2
  103.5 4.3 %collective-permute-start.6 = (f32[189,128]{0,1:T(8,128)S(1)}, f32[189,128]{0,1:T(8,128)S(1)}, u32[]{:S(2)}, u32[]{:S(2)}) collective-permute-start(f32[189,128]{0,1:T(8,128)S(1)} %get-tuple-element.40), channel_id=1, source_target_pairs={{0,256},{256,512},{512,768},{1,257},{257,513},{513,769},{2,258},{2... | collective-permute-start | bytes 290312 | tf_op jit(solution)/shard_map/ppermute | solution.py:22
  109.1 9.7 %collective-permute-start.8 = (f32[189,128]{0,1:T(8,128)S(1)}, f32[189,128]{0,1:T(8,128)S(1)}, u32[]{:S(2)}, u32[]{:S(2)}) collective-permute-start(f32[189,128]{0,1:T(8,128)S(1)} %get-tuple-element.38), channel_id=1, source_target_pairs={{0,16},{16,32},{32,48},{48,64},{64,80},{80,96},{96,112},{112,128},... | collective-permute-start | bytes 290312 | tf_op jit(solution)/shard_map/ppermute | solution.py:22
  118.7 1.9 collective-permute-start.9
  120.7 4.5 %collective-permute-start.10 = (f32[189,128]{0,1:T(8,128)S(1)}, f32[189,128]{0,1:T(8,128)S(1)}, u32[]{:S(2)}, u32[]{:S(2)}) collective-permute-start(f32[189,128]{0,1:T(8,128)S(1)} %get-tuple-element.36), channel_id=1, source_target_pairs={{0,1},{1,2},{2,3},{3,4},{4,5},{5,6},{6,7},{7,8},{8,9},{9,10},{10,1... | collective-permute-start | bytes 290312 | tf_op jit(solution)/shard_map/ppermute | solution.py:22
  125.2 1.9 collective-permute-start.11
  127.2 4.5 %collective-permute-done.9 = f32[189,128]{0,1:T(8,128)S(1)} collective-permute-done((f32[189,128]{0,1:T(8,128)S(1)}, f32[189,128]{0,1:T(8,128)S(1)}, u32[]{:S(2)}, u32[]{:S(2)}) %collective-permute-start.9) | collective-permute-done | bytes 96800 | tf_op jit(solution)/shard_map/ppermute | solution.py:22
  157.9 2.1 gather_fusion.4
  160.9 4.4 %collective-permute-start.12 = (f32[189,128]{0,1:T(8,128)S(1)}, f32[189,128]{0,1:T(8,128)S(1)}, u32[]{:S(2)}, u32[]{:S(2)}) collective-permute-start(f32[189,128]{0,1:T(8,128)S(1)} %get-tuple-element.34), channel_id=1, source_target_pairs={{0,256},{256,512},{512,768},{1,257},{257,513},{513,769},{2,258},{2... | collective-permute-start | bytes 290312 | tf_op jit(solution)/shard_map/ppermute | solution.py:22
  166.6 9.6 %collective-permute-start.14 = (f32[189,128]{0,1:T(8,128)S(1)}, f32[189,128]{0,1:T(8,128)S(1)}, u32[]{:S(2)}, u32[]{:S(2)}) collective-permute-start(f32[189,128]{0,1:T(8,128)S(1)} %get-tuple-element.32), channel_id=1, source_target_pairs={{0,16},{16,32},{32,48},{48,64},{64,80},{80,96},{96,112},{112,128},... | collective-permute-start | bytes 290312 | tf_op jit(solution)/shard_map/ppermute | solution.py:22
  176.3 1.9 collective-permute-start.15
  178.2 2.4 collective-permute-start.16
  180.6 2.0 collective-permute-start.17
  182.7 5.9 %collective-permute-done.15 = f32[189,128]{0,1:T(8,128)S(1)} collective-permute-done((f32[189,128]{0,1:T(8,128)S(1)}, f32[189,128]{0,1:T(8,128)S(1)}, u32[]{:S(2)}, u32[]{:S(2)}) %collective-permute-start.15) | collective-permute-done | bytes 96800 | tf_op jit(solution)/shard_map/ppermute | solution.py:22
  188.6 2.4 gather_fusion.5
  212.4 2.1 gather_fusion.6
  216.4 6.1 %collective-permute-start.18 = (f32[189,128]{0,1:T(8,128)}, f32[189,128]{0,1:T(8,128)}, u32[]{:S(2)}, u32[]{:S(2)}) collective-permute-start(f32[189,128]{0,1:T(8,128)} %get-tuple-element.28), channel_id=1, source_target_pairs={{0,256},{256,512},{512,768},{1,257},{257,513},{513,769},{2,258},{2... | collective-permute-start | bytes 290312 | tf_op jit(solution)/shard_map/ppermute | solution.py:22
  223.7 8.6 %collective-permute-start.20 = (f32[189,128]{0,1:T(8,128)}, f32[189,128]{0,1:T(8,128)}, u32[]{:S(2)}, u32[]{:S(2)}) collective-permute-start(f32[189,128]{0,1:T(8,128)} %get-tuple-element.26), channel_id=1, source_target_pairs={{0,16},{16,32},{32,48},{48,64},{64,80},{80,96},{96,112},{112,128},... | collective-permute-start | bytes 290312 | tf_op jit(solution)/shard_map/ppermute | solution.py:22
  232.4 1.9 collective-permute-start.21
  234.3 2.3 collective-permute-start.22
  239.3 2.0 collective-permute-start.23
  247.4 1.6 gather_fusion.7
  (454 shorter events, 119.3 us)
Async XLA Ops:
  1.4 158.6 %copy-start.64 = (pred[768]{0:T(1024)(128)(4,1)}, pred[768]{0:T(1024)(128)(4,1)S(1)}, u32[]{:S(2)}) copy-start(pred[768]{0:T(1024)(128)(4,1)S(1)} %compare_and_fusion) | copy-start | bytes 2308
  15.5 142.4 %copy-start.58 = (s32[1024]{0:T(1024)}, s32[1024]{0:T(1024)S(1)}, u32[]{:S(2)}) copy-start(s32[1024]{0:T(1024)S(1)} %pad_clamp_fusion.1) | copy-start | bytes 12292
  15.6 87.6 %copy-start.66 = (pred[6,128]{1,0:T(8,128)(4,1)}, pred[6,128]{1,0:T(8,128)(4,1)S(1)}, u32[]{:S(2)}) copy-start(pred[6,128]{1,0:T(8,128)(4,1)S(1)} %iota_compare_fusion.1) | copy-start | bytes 2308
  19.0 27.4 %copy-start.78 = (s32[4,128]{1,0:T(4,128)S(1)}, s32[4,128]{1,0:T(4,128)}, u32[]{:S(2)}) copy-start(s32[4,128]{1,0:T(4,128)} %param.28) | copy-start | bytes 6148
  19.0 29.2 %copy-start.90 = (s32[128]{0:T(128)S(1)}, s32[128]{0:T(128)}, u32[]{:S(2)}) copy-start(s32[128]{0:T(128)} %get-tuple-element.57) | copy-start | bytes 1540
  19.0 30.3 %copy-start.37 = (f32[3,56,56]{2,1,0:T(8,128)S(1)}, f32[3,56,56]{2,1,0:T(8,128)}, u32[]{:S(2)}) copy-start(f32[3,56,56]{2,1,0:T(8,128)} %param.21) | copy-start | bytes 112900
  19.0 36.7 %collective-permute-start = (f32[189,128]{0,1:T(8,128)}, f32[189,128]{0,1:T(8,128)}, u32[]{:S(2)}, u32[]{:S(2)}) collective-permute-start(f32[189,128]{0,1:T(8,128)} %get-tuple-element.46), channel_id=1, source_target_pairs={{0,256},{256,512},{512,768},{1,257},{257,513},{513,769},{2,258},{2... | collective-permute-start | bytes 290312 | tf_op jit(solution)/shard_map/ppermute | solution.py:22
  24.7 33.9 %collective-permute-start.1 = (f32[189,128]{0,1:T(8,128)}, f32[189,128]{0,1:T(8,128)}, u32[]{:S(2)}, u32[]{:S(2)}) collective-permute-start(f32[189,128]{0,1:T(8,128)} %get-tuple-element.45), channel_id=1, source_target_pairs={{256,0},{512,256},{768,512},{257,1},{513,257},{769,513},{258,2},{5... | collective-permute-start | bytes 290312 | tf_op jit(solution)/shard_map/ppermute | solution.py:22
  26.0 33.5 %collective-permute-start.2 = (f32[189,128]{0,1:T(8,128)}, f32[189,128]{0,1:T(8,128)}, u32[]{:S(2)}, u32[]{:S(2)}) collective-permute-start(f32[189,128]{0,1:T(8,128)} %get-tuple-element.44), channel_id=1, source_target_pairs={{0,16},{16,32},{32,48},{48,64},{64,80},{80,96},{96,112},{112,128},... | collective-permute-start | bytes 290312 | tf_op jit(solution)/shard_map/ppermute | solution.py:22
  37.8 22.6 %collective-permute-start.3 = (f32[189,128]{0,1:T(8,128)}, f32[189,128]{0,1:T(8,128)}, u32[]{:S(2)}, u32[]{:S(2)}) collective-permute-start(f32[189,128]{0,1:T(8,128)} %get-tuple-element.43), channel_id=1, source_target_pairs={{16,0},{32,16},{48,32},{64,48},{80,64},{96,80},{112,96},{128,112},... | collective-permute-start | bytes 290312 | tf_op jit(solution)/shard_map/ppermute | solution.py:22
  39.7 21.6 %collective-permute-start.4 = (f32[189,128]{0,1:T(8,128)}, f32[189,128]{0,1:T(8,128)}, u32[]{:S(2)}, u32[]{:S(2)}) collective-permute-start(f32[189,128]{0,1:T(8,128)} %get-tuple-element.42), channel_id=1, source_target_pairs={{0,1},{1,2},{2,3},{3,4},{4,5},{5,6},{6,7},{7,8},{8,9},{9,10},{10,1... | collective-permute-start | bytes 290312 | tf_op jit(solution)/shard_map/ppermute | solution.py:22
  55.7 132.9 %copy-start.61 = (s32[1024]{0:T(1024)}, s32[1024]{0:T(1024)S(1)}, u32[]{:S(2)}) copy-start(s32[1024]{0:T(1024)S(1)} %pad_clamp_fusion) | copy-start | bytes 12292
  55.7 7.5 %collective-permute-start.5 = (f32[189,128]{0,1:T(8,128)S(1)}, f32[189,128]{0,1:T(8,128)S(1)}, u32[]{:S(2)}, u32[]{:S(2)}) collective-permute-start(f32[189,128]{0,1:T(8,128)S(1)} %copy-done.56), channel_id=1, source_target_pairs={{1,0},{2,1},{3,2},{4,3},{5,4},{6,5},{7,6},{8,7},{9,8},{10,9},{11,1... | collective-permute-start | bytes 290312 | tf_op jit(solution)/shard_map/ppermute | solution.py:22
  103.5 21.7 %collective-permute-start.6 = (f32[189,128]{0,1:T(8,128)S(1)}, f32[189,128]{0,1:T(8,128)S(1)}, u32[]{:S(2)}, u32[]{:S(2)}) collective-permute-start(f32[189,128]{0,1:T(8,128)S(1)} %get-tuple-element.40), channel_id=1, source_target_pairs={{0,256},{256,512},{512,768},{1,257},{257,513},{513,769},{2,258},{2... | collective-permute-start | bytes 290312 | tf_op jit(solution)/shard_map/ppermute | solution.py:22
  107.8 19.4 %collective-permute-start.7 = (f32[189,128]{0,1:T(8,128)S(1)}, f32[189,128]{0,1:T(8,128)S(1)}, u32[]{:S(2)}, u32[]{:S(2)}) collective-permute-start(f32[189,128]{0,1:T(8,128)S(1)} %get-tuple-element.39), channel_id=1, source_target_pairs={{256,0},{512,256},{768,512},{257,1},{513,257},{769,513},{258,2},{5... | collective-permute-start | bytes 290312 | tf_op jit(solution)/shard_map/ppermute | solution.py:22
  109.1 18.1 %collective-permute-start.8 = (f32[189,128]{0,1:T(8,128)S(1)}, f32[189,128]{0,1:T(8,128)S(1)}, u32[]{:S(2)}, u32[]{:S(2)}) collective-permute-start(f32[189,128]{0,1:T(8,128)S(1)} %get-tuple-element.38), channel_id=1, source_target_pairs={{0,16},{16,32},{32,48},{48,64},{64,80},{80,96},{96,112},{112,128},... | collective-permute-start | bytes 290312 | tf_op jit(solution)/shard_map/ppermute | solution.py:22
  118.7 13.0 %collective-permute-start.9 = (f32[189,128]{0,1:T(8,128)S(1)}, f32[189,128]{0,1:T(8,128)S(1)}, u32[]{:S(2)}, u32[]{:S(2)}) collective-permute-start(f32[189,128]{0,1:T(8,128)S(1)} %get-tuple-element.37), channel_id=1, source_target_pairs={{16,0},{32,16},{48,32},{64,48},{80,64},{96,80},{112,96},{128,112},... | collective-permute-start | bytes 290312 | tf_op jit(solution)/shard_map/ppermute | solution.py:22
  120.7 11.1 %collective-permute-start.10 = (f32[189,128]{0,1:T(8,128)S(1)}, f32[189,128]{0,1:T(8,128)S(1)}, u32[]{:S(2)}, u32[]{:S(2)}) collective-permute-start(f32[189,128]{0,1:T(8,128)S(1)} %get-tuple-element.36), channel_id=1, source_target_pairs={{0,1},{1,2},{2,3},{3,4},{4,5},{5,6},{6,7},{7,8},{8,9},{9,10},{10,1... | collective-permute-start | bytes 290312 | tf_op jit(solution)/shard_map/ppermute | solution.py:22
  125.2 7.5 %collective-permute-start.11 = (f32[189,128]{0,1:T(8,128)S(1)}, f32[189,128]{0,1:T(8,128)S(1)}, u32[]{:S(2)}, u32[]{:S(2)}) collective-permute-start(f32[189,128]{0,1:T(8,128)S(1)} %get-tuple-element.35), channel_id=1, source_target_pairs={{1,0},{2,1},{3,2},{4,3},{5,4},{6,5},{7,6},{8,7},{9,8},{10,9},{11,1... | collective-permute-start | bytes 290312 | tf_op jit(solution)/shard_map/ppermute | solution.py:22
  160.9 19.7 %collective-permute-start.12 = (f32[189,128]{0,1:T(8,128)S(1)}, f32[189,128]{0,1:T(8,128)S(1)}, u32[]{:S(2)}, u32[]{:S(2)}) collective-permute-start(f32[189,128]{0,1:T(8,128)S(1)} %get-tuple-element.34), channel_id=1, source_target_pairs={{0,256},{256,512},{512,768},{1,257},{257,513},{513,769},{2,258},{2... | collective-permute-start | bytes 290312 | tf_op jit(solution)/shard_map/ppermute | solution.py:22
  165.3 17.3 %collective-permute-start.13 = (f32[189,128]{0,1:T(8,128)S(1)}, f32[189,128]{0,1:T(8,128)S(1)}, u32[]{:S(2)}, u32[]{:S(2)}) collective-permute-start(f32[189,128]{0,1:T(8,128)S(1)} %get-tuple-element.33), channel_id=1, source_target_pairs={{256,0},{512,256},{768,512},{257,1},{513,257},{769,513},{258,2},{5... | collective-permute-start | bytes 290312 | tf_op jit(solution)/shard_map/ppermute | solution.py:22
  166.6 16.0 %collective-permute-start.14 = (f32[189,128]{0,1:T(8,128)S(1)}, f32[189,128]{0,1:T(8,128)S(1)}, u32[]{:S(2)}, u32[]{:S(2)}) collective-permute-start(f32[189,128]{0,1:T(8,128)S(1)} %get-tuple-element.32), channel_id=1, source_target_pairs={{0,16},{16,32},{32,48},{48,64},{64,80},{80,96},{96,112},{112,128},... | collective-permute-start | bytes 290312 | tf_op jit(solution)/shard_map/ppermute | solution.py:22
  176.3 12.3 %collective-permute-start.15 = (f32[189,128]{0,1:T(8,128)S(1)}, f32[189,128]{0,1:T(8,128)S(1)}, u32[]{:S(2)}, u32[]{:S(2)}) collective-permute-start(f32[189,128]{0,1:T(8,128)S(1)} %get-tuple-element.31), channel_id=1, source_target_pairs={{16,0},{32,16},{48,32},{64,48},{80,64},{96,80},{112,96},{128,112},... | collective-permute-start | bytes 290312 | tf_op jit(solution)/shard_map/ppermute | solution.py:22
  178.2 10.4 %collective-permute-start.16 = (f32[189,128]{0,1:T(8,128)S(1)}, f32[189,128]{0,1:T(8,128)S(1)}, u32[]{:S(2)}, u32[]{:S(2)}) collective-permute-start(f32[189,128]{0,1:T(8,128)S(1)} %get-tuple-element.30), channel_id=1, source_target_pairs={{0,1},{1,2},{2,3},{3,4},{4,5},{5,6},{6,7},{7,8},{8,9},{9,10},{10,1... | collective-permute-start | bytes 290312 | tf_op jit(solution)/shard_map/ppermute | solution.py:22
  180.6 8.0 %collective-permute-start.17 = (f32[189,128]{0,1:T(8,128)S(1)}, f32[189,128]{0,1:T(8,128)S(1)}, u32[]{:S(2)}, u32[]{:S(2)}) collective-permute-start(f32[189,128]{0,1:T(8,128)S(1)} %get-tuple-element.29), channel_id=1, source_target_pairs={{1,0},{2,1},{3,2},{4,3},{5,4},{6,5},{7,6},{8,7},{9,8},{10,9},{11,1... | collective-permute-start | bytes 290312 | tf_op jit(solution)/shard_map/ppermute | solution.py:22
  215.2 21.4 %copy-start.47 = (f32[9,7,8,128]{3,2,1,0:T(8,128)S(1)}, f32[9,7,8,128]{3,2,1,0:T(8,128)}, u32[]{:S(2)}) copy-start(f32[9,7,8,128]{3,2,1,0:T(8,128)} %get-tuple-element.9) | copy-start | bytes 774148
  216.4 23.0 %collective-permute-start.18 = (f32[189,128]{0,1:T(8,128)}, f32[189,128]{0,1:T(8,128)}, u32[]{:S(2)}, u32[]{:S(2)}) collective-permute-start(f32[189,128]{0,1:T(8,128)} %get-tuple-element.28), channel_id=1, source_target_pairs={{0,256},{256,512},{512,768},{1,257},{257,513},{513,769},{2,258},{2... | collective-permute-start | bytes 290312 | tf_op jit(solution)/shard_map/ppermute | solution.py:22
  222.4 19.8 %collective-permute-start.19 = (f32[189,128]{0,1:T(8,128)}, f32[189,128]{0,1:T(8,128)}, u32[]{:S(2)}, u32[]{:S(2)}) collective-permute-start(f32[189,128]{0,1:T(8,128)} %get-tuple-element.27), channel_id=1, source_target_pairs={{256,0},{512,256},{768,512},{257,1},{513,257},{769,513},{258,2},{5... | collective-permute-start | bytes 290312 | tf_op jit(solution)/shard_map/ppermute | solution.py:22
  223.7 19.5 %collective-permute-start.20 = (f32[189,128]{0,1:T(8,128)}, f32[189,128]{0,1:T(8,128)}, u32[]{:S(2)}, u32[]{:S(2)}) collective-permute-start(f32[189,128]{0,1:T(8,128)} %get-tuple-element.26), channel_id=1, source_target_pairs={{0,16},{16,32},{32,48},{48,64},{64,80},{80,96},{96,112},{112,128},... | collective-permute-start | bytes 290312 | tf_op jit(solution)/shard_map/ppermute | solution.py:22
  232.4 13.1 %collective-permute-start.21 = (f32[189,128]{0,1:T(8,128)}, f32[189,128]{0,1:T(8,128)}, u32[]{:S(2)}, u32[]{:S(2)}) collective-permute-start(f32[189,128]{0,1:T(8,128)} %get-tuple-element.25), channel_id=1, source_target_pairs={{16,0},{32,16},{48,32},{64,48},{80,64},{96,80},{112,96},{128,112},... | collective-permute-start | bytes 290312 | tf_op jit(solution)/shard_map/ppermute | solution.py:22
  234.3 12.1 %collective-permute-start.22 = (f32[189,128]{0,1:T(8,128)}, f32[189,128]{0,1:T(8,128)}, u32[]{:S(2)}, u32[]{:S(2)}) collective-permute-start(f32[189,128]{0,1:T(8,128)} %get-tuple-element.24), channel_id=1, source_target_pairs={{0,1},{1,2},{2,3},{3,4},{4,5},{5,6},{6,7},{7,8},{8,9},{9,10},{10,1... | collective-permute-start | bytes 290312 | tf_op jit(solution)/shard_map/ppermute | solution.py:22
  239.3 8.0 %collective-permute-start.23 = (f32[189,128]{0,1:T(8,128)S(1)}, f32[189,128]{0,1:T(8,128)S(1)}, u32[]{:S(2)}, u32[]{:S(2)}) collective-permute-start(f32[189,128]{0,1:T(8,128)S(1)} %copy-done.57), channel_id=1, source_target_pairs={{1,0},{2,1},{3,2},{4,3},{5,4},{6,5},{7,6},{8,7},{9,8},{10,9},{11,1... | collective-permute-start | bytes 290312 | tf_op jit(solution)/shard_map/ppermute | solution.py:22
  (99 other events, 298.0 us)
where the time goes:
time: 257 us; the launch traced here: 254 us
  starting transfers between devices  95.7 us (37%)
  local copies, waits for them, and re-layouts  55.6 us (22%)
  other arithmetic  53.6 us (21%)
  matrix products  32.6 us (13%)
  waiting for transfers between devices  13.7 us (5%)
  between operations  2.95 us (1%)
    ppermute x24, starting transfers between devices, shifted(): lax.ppermute(value, axis, [(source, source + steps) for source in range(l...  95.7 us
    reduce_sum x20, other arithmetic, derivative_terms(): current = -jnp.sum(small_apply(mixed_terms, jacobians), axis=0)  26.5 us
    unnamed x240, local copies, waits for them, and re-layouts  18.9 us
    dot_general x20, matrix products, derivative_terms(): jnp.dot(stiff_stack, current.reshape(BASIS, -1), precision=highest)  17.5 us
    ppermute x24, waiting for transfers between devices, shifted(): lax.ppermute(value, axis, [(source, source + steps) for source in range(l...  13.7 us
    mul x46, local copies, waits for them, and re-layouts, small_apply(): values[:, :, :, None, :] * matrices[:, None, :, :, :]  10.1 us
    gather x4, local copies, waits for them, and re-layouts, local(): jnp.take(own_table, send_flat, axis=1).reshape(block_width, 6, slot_count)  8.43 us
    gather x4, local copies, waits for them, and re-layouts, local(): gathered = jnp.take(face_table, neighbour_flat, axis=1)  7.1 us
  transfers between devices with their start and end apart: 24, of which 5 were waited for; matrix products, arithmetic and copies ran while one was open for 9% of the time, Pallas kernels for 0%

commit v1 on v0

v1 whole, which is shorter than its diff:
```python
import jax
import jax.numpy as jnp
from jax import lax
from jax.experimental import pallas as pl
from jax.experimental.pallas import tpu as pltpu
from jax.sharding import PartitionSpec as P

BASIS = 56
QUANTITIES = 9
FACE_BASIS = 21
DERIVATIVES = 6
SUBSTEPS = 4
LANES = 128
FACES = 4
DIRECTIONS = 6
FACE_ROWS = 24
PACKED = 192
MESH = pl.DeviceIdType.MESH
AXES = ("gx", "gy", "gz")

f32 = jnp.float32
bf16 = jnp.bfloat16


def halves(value):
    high = value.astype(bf16).astype(f32)
    return high, value - high


def stacked(value):
    high, low = halves(value)
    return jnp.concatenate([high, low, high], axis=0).astype(bf16)


def place(rows, columns, offsets):
    row = lax.broadcasted_iota(jnp.int32, (rows, columns), 0)
    column = lax.broadcasted_iota(jnp.int32, (rows, columns), 1)
    hit = column == row + offsets[0]
    for offset in offsets[1:]:
        hit = hit | (column == row + offset)
    return jnp.where(hit, 1.0, 0.0).astype(bf16)


def widened(matrix, columns, first, second, third):
    high, low = halves(matrix)
    depth = matrix.shape[1]
    return jnp.dot(
        high.astype(bf16), place(depth, columns, (first, second)), preferred_element_type=f32
    ) + jnp.dot(low.astype(bf16), place(depth, columns, (third,)), preferred_element_type=f32)


def dot(left, right):
    return jnp.dot(left, right, preferred_element_type=f32)


def kernel(
    sol_ref, jac_ref, ds_ref, vs_ref, fp_ref, fl_ref, fr_ref, ls_ref, ns_ref,
    cluster_ref, neigh_ref, orient_ref, faces_ref, counts_ref, out_ref,
    cur, own, flux, integ, mixed, volume, operand, projected, table, pair,
    inner, total, chosen, zface, zstack, jac_b, ls_b, ns_b, weights,
    d_mat, v_mat, p_mat, l_mat, r_mat, build, build2, send_hot, recv_hot,
    send_buf, recv_buf, send_sem, recv_sem,
):
    index = [lax.axis_index(name) for name in AXES]
    count = [lax.axis_size(name) for name in AXES]
    has_lower = [index[a] > 0 for a in range(3)]
    has_higher = [index[a] < count[a] - 1 for a in range(3)]

    barrier = pltpu.get_barrier_semaphore()
    arrivals = jnp.int32(0)
    for a in range(3):
        for there, step in ((has_lower[a], -1), (has_higher[a], 1)):
            arrivals = arrivals + there.astype(jnp.int32)

            @pl.when(there)
            def _(a=a, step=step):
                pl.semaphore_signal(
                    barrier, inc=1, device_id={AXES[a]: index[a] + step}, device_id_type=MESH
                )

    for d in range(3):
        for q in range(QUANTITIES):
            for p in range(QUANTITIES):
                jac_b[(d * 9 + q) * 9 + p] = jnp.broadcast_to(jac_ref[d, q, p : p + 1, :], (8, LANES))
    d_mat[...] = widened(-ds_ref[...].reshape(3 * BASIS, BASIS), 3 * BASIS, 0, BASIS, 2 * BASIS).astype(bf16)
    for q in range(QUANTITIES):
        cur[q] = sol_ref[:, q, :]
        own[q] = jnp.zeros((BASIS, LANES), f32)
        flux[q] = jnp.zeros((BASIS, LANES), f32)
    build[...] = jnp.zeros_like(build)
    for j in range(FACES):
        build[j * FACE_ROWS : j * FACE_ROWS + FACE_BASIS, :] = widened(
            fp_ref[j], 3 * BASIS, 0, BASIS, 2 * BASIS
        )
    p_mat[...] = build[...].astype(bf16)
    slot = lax.broadcasted_iota(jnp.int32, (1, LANES), 1)
    face_row = lax.broadcasted_iota(jnp.int32, (FACES * LANES, LANES), 0)
    for k in range(DIRECTIONS):
        named = jnp.where(slot < counts_ref[k : k + 1, :], faces_ref[k : k + 1, :], -1)
        send_hot[:, k * LANES : (k + 1) * LANES] = jnp.where(face_row == named, 1.0, 0.0).astype(bf16)
    for a in range(3):
        for s in range(2):

            @pl.when(jnp.logical_not((has_lower, has_higher)[s][a]))
            def _(k=2 * a + s):
                for step in range(SUBSTEPS):
                    recv_buf[step, k] = jnp.zeros((PACKED, LANES), f32)

    def late_constants():
        block_row = lax.broadcasted_iota(jnp.int32, ((FACES + DIRECTIONS) * LANES, LANES), 0)
        for i in range(FACES):
            recv_hot[:, i * LANES : (i + 1) * LANES] = jnp.where(
                block_row == neigh_ref[i : i + 1, :], 1.0, 0.0
            ).astype(bf16)
        for i in range(FACES):
            for q in range(QUANTITIES):
                for p in range(QUANTITIES):
                    at = (i * 9 + q) * 9 + p
                    ls_b[at] = jnp.broadcast_to(ls_ref[i, q, p : p + 1, :], (8, LANES))
                    ns_b[at] = jnp.broadcast_to(ns_ref[i, q, p : p + 1, :], (8, LANES))
        v_mat[...] = widened(vs_ref[...].reshape(3 * BASIS, BASIS), 3 * BASIS, 0, BASIS, 2 * BASIS).astype(bf16)
        width = FACES * FACE_ROWS
        joined = jnp.zeros((BASIS, 3 * width), f32)
        for i in range(FACES):
            at = i * FACE_ROWS
            joined = joined + widened(fl_ref[i], 3 * width, at, width + at, 2 * width + at)
        l_mat[...] = joined.astype(bf16)
        build2[...] = jnp.zeros_like(build2)
        for o in range(3):
            build2[o * FACE_ROWS : o * FACE_ROWS + FACE_BASIS, :] = widened(
                fr_ref[o], 3 * FACE_ROWS, 0, FACE_ROWS, 2 * FACE_ROWS
            )
        r_mat[...] = build2[...].astype(bf16)

    late_constants()

    def columns(q, width=1):
        return slice(q * LANES, (q + width) * LANES)

    def mix(matrix):
        left = matrix[...]
        for q in range(0, QUANTITIES, 2):
            width = min(2, QUANTITIES - q)
            product = dot(left, operand[:, columns(q, width)])
            for w in range(width):
                mixed[q + w] = product[:, columns(w)]

    def apply_jacobians(sink):
        for p0 in range(0, QUANTITIES, 3):
            sums = [None] * 3
            for d in range(3):
                for q in range(QUANTITIES):
                    part = mixed[q, d * BASIS : (d + 1) * BASIS, :].reshape(7, 8, LANES)
                    for w in range(3):
                        term = part * jac_b[(d * 9 + q) * 9 + p0 + w][None]
                        sums[w] = term if sums[w] is None else sums[w] + term
            for w in range(3):
                sink(p0 + w, sums[w].reshape(BASIS, LANES))

    def copy(s, k):
        a, side = k // 2, k % 2
        return pltpu.make_async_remote_copy(
            src_ref=send_buf.at[s, k],
            dst_ref=recv_buf.at[s, k],
            send_sem=send_sem.at[s, k],
            recv_sem=recv_sem.at[s, k],
            device_id={AXES[a]: index[a] + (1, -1)[side]},
            device_id_type=MESH,
        )

    def sends(k):
        return (has_higher, has_lower)[k % 2][k // 2]

    def receives(k):
        return (has_lower, has_higher)[k % 2][k // 2]

    period = jnp.left_shift(jnp.ones((8, LANES), jnp.int32), jnp.broadcast_to(cluster_ref[...], (8, LANES)))

    def substep(s, carry):
        offset_int = s & (period - 1)
        ending = ((s + 1) & (period - 1)) == 0
        offset = offset_int.astype(f32)
        upper, lower = (offset + 1.0) * 0.25, offset * 0.25
        up, low, factorial = upper, lower, 1.0
        for m in range(DERIVATIVES):
            factorial = factorial * (m + 1)
            weights[m] = (up - low) * (1.0 / factorial)
            up, low = up * upper, low * lower

        for q in range(QUANTITIES):
            value = cur[q]
            operand[:, columns(q)] = stacked(value)
            integ[q] = (value.reshape(7, 8, LANES) * weights[0][None]).reshape(BASIS, LANES)

        def derivative(m, carry):
            mix(d_mat)
            weight = weights[m]

            def sink(p, value):
                operand[:, columns(p)] = stacked(value)
                integ[p] = integ[p] + (value.reshape(7, 8, LANES) * weight[None]).reshape(BASIS, LANES)

            apply_jacobians(sink)
            return carry

        lax.fori_loop(1, DERIVATIVES, derivative, 0)

        for q in range(QUANTITIES):
            operand[:, columns(q)] = stacked(integ[q])
        for q in range(0, QUANTITIES, 2):
            width = min(2, QUANTITIES - q)
            product = dot(p_mat[...], operand[:, columns(q, width)])
            for w in range(width):
                projected[q + w] = product[:, columns(w)]
        for q in range(QUANTITIES):
            for j in range(FACES):
                table[j, q * FACE_BASIS : q * FACE_BASIS + FACE_ROWS, :] = projected[
                    q, j * FACE_ROWS : (j + 1) * FACE_ROWS, :
                ]
        for j in range(FACES):
            high, low = halves(table[j])
            pair[0:PACKED, columns(j)] = high.astype(bf16)
            pair[PACKED : 2 * PACKED, columns(j)] = low.astype(bf16)

        for a in (1, 0, 2):
            product = dot(pair[:, 0 : FACES * LANES], send_hot[:, columns(2 * a, 2)])
            product = product[0:PACKED] + product[PACKED : 2 * PACKED]
            for side in range(2):
                k = 2 * a + side
                send_buf[s, k] = product[:, columns(side)]

        @pl.when(s == 0)
        def _():
            pl.semaphore_wait(barrier, arrivals)

        for k in (2, 3, 0, 1, 4, 5):

            @pl.when(sends(k))
            def _(k=k):
                copy(s, k).start()

        for i in range(0, FACES, 2):
            product = dot(pair[:, 0 : FACES * LANES], recv_hot[0 : FACES * LANES, columns(i, 2)])
            product = product[0:PACKED] + product[PACKED : 2 * PACKED]
            inner[i] = product[:, columns(0)]
            inner[i + 1] = product[:, columns(1)]

        def solve(i, blocks, solver, sink):
            for p0 in range(0, QUANTITIES, 3):
                sums = [None] * 3
                for q in range(QUANTITIES):
                    part = blocks(q).reshape(3, 8, LANES)
                    for w in range(3):
                        term = part * solver[(i * 9 + q) * 9 + p0 + w][None]
                        sums[w] = term if sums[w] is None else sums[w] + term
                for w in range(3):
                    sink(p0 + w, sums[w].reshape(FACE_ROWS, LANES))

        for i in range(FACES):
            rows = slice(i * FACE_ROWS, (i + 1) * FACE_ROWS)

            def keep(p, value, rows=rows):
                zface[p, rows, :] = value

            solve(i, lambda q, rows=rows: projected[q, rows, :], ls_b, keep)

        for q in range(QUANTITIES):
            value = own[q] + integ[q]
            own[q] = value
            operand[:, columns(q)] = stacked(value)
        mix(v_mat)

        def keep_volume(p, value):
            volume[p] = value

        apply_jacobians(keep_volume)

        for k in (4, 5, 0, 1, 2, 3):

            @pl.when(receives(k))
            def _(k=k):
                copy(s, k).wait_recv()

        for k in range(DIRECTIONS):
            high, low = halves(recv_buf[s, k])
            pair[0:PACKED, columns(k)] = high.astype(bf16)
            pair[PACKED : 2 * PACKED, columns(k)] = low.astype(bf16)
        for i in range(0, FACES, 2):
            product = dot(pair[...], recv_hot[FACES * LANES :, columns(i, 2)])
            product = product[0:PACKED] + product[PACKED : 2 * PACKED]
            total[i] = inner[i] + product[:, columns(0)]
            total[i + 1] = inner[i + 1] + product[:, columns(1)]

        for i in range(FACES):
            rows = slice(i * FACE_ROWS, (i + 1) * FACE_ROWS)
            turn = jnp.broadcast_to(orient_ref[i : i + 1, :], (8, LANES))[None]
            for q in range(QUANTITIES):
                zstack[0 : 3 * FACE_ROWS, columns(q)] = stacked(
                    total[i, q * FACE_BASIS : q * FACE_BASIS + FACE_ROWS, :]
                )
            for q in range(0, QUANTITIES, 2):
                width = min(2, QUANTITIES - q)
                product = dot(r_mat[...], zstack[0 : 3 * FACE_ROWS, columns(q, width)])
                for w in range(width):
                    parts = [
                        product[o * FACE_ROWS : (o + 1) * FACE_ROWS, columns(w)].reshape(3, 8, LANES)
                        for o in range(3)
                    ]
                    picked = jnp.where(turn == 0, parts[0], jnp.where(turn == 1, parts[1], parts[2]))
                    chosen[q + w] = picked.reshape(FACE_ROWS, LANES)

            def add(p, value, rows=rows):
                zface[p, rows, :] = zface[p, rows, :] + value

            solve(i, lambda q: chosen[q], ns_b, add)

        for p in range(QUANTITIES):
            zstack[:, columns(p)] = stacked(zface[p])
        for p in range(0, QUANTITIES, 2):
            width = min(2, QUANTITIES - p)
            product = dot(l_mat[...], zstack[:, columns(p, width)])
            for w in range(width):
                at = p + w
                done = ending[None]
                fluxes = (flux[at] + product[:, columns(w)]).reshape(7, 8, LANES)
                old = cur[at].reshape(7, 8, LANES)
                fresh = old + volume[at].reshape(7, 8, LANES) - fluxes
                cur[at] = jnp.where(done, fresh, old).reshape(BASIS, LANES)
                flux[at] = jnp.where(done, 0.0, fluxes).reshape(BASIS, LANES)
                own[at] = jnp.where(done, 0.0, own[at].reshape(7, 8, LANES)).reshape(BASIS, LANES)
        return carry

    lax.fori_loop(0, SUBSTEPS, substep, 0)

    for s in range(SUBSTEPS):
        for k in range(DIRECTIONS):

            @pl.when(sends(k))
            def _(s=s, k=k):
                copy(s, k).wait_send()

    for q in range(QUANTITIES):
        out_ref[:, q, :] = cur[q]


def local(*arrays):
    arrays = list(arrays)
    arrays[9] = arrays[9].reshape(1, LANES)
    width = QUANTITIES * LANES
    state = pltpu.VMEM((QUANTITIES, BASIS, LANES), f32)
    vmem = pltpu.VMEM
    return pl.pallas_call(
        kernel,
        out_shape=jax.ShapeDtypeStruct((BASIS, QUANTITIES, LANES), f32),
        in_specs=[pl.BlockSpec(memory_space=pltpu.VMEM)] * len(arrays),
        out_specs=pl.BlockSpec(memory_space=pltpu.VMEM),
        scratch_shapes=[
            state,
            state,
            state,
            state,
            vmem((QUANTITIES, 3 * BASIS, LANES), f32),
            state,
            vmem((3 * BASIS, width), bf16),
            vmem((QUANTITIES, FACES * FACE_ROWS, LANES), f32),
            vmem((FACES, PACKED, LANES), f32),
            vmem((2 * PACKED, DIRECTIONS * LANES), bf16),
            vmem((FACES, PACKED, LANES), f32),
            vmem((FACES, PACKED, LANES), f32),
            vmem((QUANTITIES, FACE_ROWS, LANES), f32),
            vmem((QUANTITIES, FACES * FACE_ROWS, LANES), f32),
            vmem((3 * FACES * FACE_ROWS, width), bf16),
            vmem((3 * 81, 8, LANES), f32),
            vmem((4 * 81, 8, LANES), f32),
            vmem((4 * 81, 8, LANES), f32),
            vmem((DERIVATIVES, 8, LANES), f32),
            vmem((3 * BASIS, 3 * BASIS), bf16),
            vmem((3 * BASIS, 3 * BASIS), bf16),
            vmem((FACES * FACE_ROWS, 3 * BASIS), bf16),
            vmem((BASIS, 3 * FACES * FACE_ROWS), bf16),
            vmem((3 * FACE_ROWS, 3 * FACE_ROWS), bf16),
            vmem((FACES * FACE_ROWS, 3 * BASIS), f32),
            vmem((3 * FACE_ROWS, 3 * FACE_ROWS), f32),
            vmem((FACES * LANES, DIRECTIONS * LANES), bf16),
            vmem(((FACES + DIRECTIONS) * LANES, FACES * LANES), bf16),
            vmem((SUBSTEPS, DIRECTIONS, PACKED, LANES), f32),
            vmem((SUBSTEPS, DIRECTIONS, PACKED, LANES), f32),
            pltpu.SemaphoreType.DMA((SUBSTEPS, DIRECTIONS)),
            pltpu.SemaphoreType.DMA((SUBSTEPS, DIRECTIONS)),
        ],
        compiler_params=pltpu.CompilerParams(
            collective_id=0, has_side_effects=True, vmem_limit_bytes=56 * 1024 * 1024
        ),
    )(*arrays)


def solution(mesh):
    spread = ("gx", "gy", "gz")
    return jax.shard_map(
        local,
        mesh=mesh,
        in_specs=(
            P(None, None, spread),
            P(None, None, None, spread),
            P(),
            P(),
            P(),
            P(),
            P(),
            P(None, None, None, spread),
            P(None, None, None, spread),
            P(spread),
            P(None, spread),
            P(None, spread),
            P(None, spread),
            P(None, spread),
        ),
        out_specs=P(None, None, spread),
        check_vma=False,
    )
```

time: 257 us -> 75.7 us (0.29)
  the two profiles are of different devices: /device:TPU:119 before, /device:TPU:240 now
where the time goes in v1:
time: 75.7 us; the launch traced here: 75.3 us
  Pallas kernels  65.4 us (86%)
  local copies, waits for them, and re-layouts  9.92 us (13%)
    pallas_call x1, Pallas kernels, local(): pl.pallas_call(kernel, out_shape=jax.ShapeDtypeStruct((BASIS, QUANTITIES,...  65.4 us
    unnamed x17, local copies, waits for them, and re-layouts  8.12 us
    pallas_call x1, local copies, waits for them, and re-layouts, local(): pl.pallas_call(kernel, out_shape=jax.ShapeDtypeStruct((BASIS, QUANTITIES,...  1.8 us

profile of v1, /device:TPU:240, one launch (start us, length us, event | category | flops | bytes accessed | tf_op | source)
XLA Modules:
  0.0 75.3 jit_solution(8931320761239046658)
XLA Ops:
  0.0 0.0 copy-start.4
  0.0 0.0 copy-start.3
  0.0 0.7 copy-done.4
  0.7 0.7 copy.21.counts_ref
  1.3 1.4 %copy.17.fp_ref = f32[4,21,56]{2,1,0:T(8,128)} copy(f32[4,21,56]{2,0,1:T(4,128)} %param.18) | data formatting | bytes 37632 | tf_op args[4]
  2.7 1.5 %copy.18.fl_ref = f32[4,56,21]{2,1,0:T(8,128)} copy(f32[4,56,21]{1,0,2:T(4,128)} %param.19) | data formatting | bytes 37632 | tf_op args[5]
  4.2 0.0 copy-done.3
  4.3 0.0 copy-start.1
  4.3 0.7 copy.16.jac_ref
  5.0 0.3 copy-done.1
  5.3 0.0 copy-start.2
  5.3 0.8 %copy.19.ls_ref = f32[4,9,9,128]{3,2,1,0:T(8,128)} copy(f32[4,9,9,128]{3,0,2,1:T(4,128)S(1)} %copy-done.1) | data formatting | bytes 331776 | tf_op args[7]
  6.0 0.2 copy-done.2
  6.2 0.0 copy-start
  6.2 0.8 %copy.20.ns_ref = f32[4,9,9,128]{3,2,1,0:T(8,128)} copy(f32[4,9,9,128]{3,0,2,1:T(4,128)S(1)} %copy-done.2) | data formatting | bytes 331776 | tf_op args[8]
  7.0 0.3 copy-done
  7.3 0.8 %copy.15.sol_ref = f32[56,9,128]{2,1,0:T(8,128)} copy(f32[56,9,128]{2,0,1:T(8,128)S(1)} %copy-done) | data formatting | bytes 516096 | tf_op args[0]
  8.1 65.4 %shard_map.136 = f32[56,9,128]{2,1,0:T(8,128)} custom-call(f32[56,9,128]{2,1,0:T(8,128)} %copy.15.sol_ref, f32[3,9,9,128]{3,2,1,0:T(8,128)} %copy.16.jac_ref, f32[3,56,56]{2,1,0:T(8,128)} %ds_ref.1, f32[3,56,56]{2,1,0:T(8,128)} %vs_ref.1, f32[4,21,56]{2,1,0:T(8,128)} %copy.17.fp_ref, f32[4,56,21]{2,1,0:T(8,128)} %copy.18.fl_ref, f32[3,21,21]{2,1,0:T(8,128)} %fr_ref.1, ...), custom_call_target="tpu_custom_call" | custom-call | tf_op jit(solution)/shard_map/pallas_call | solution.py:352
  73.5 1.8 %copy.22 = f32[56,9,128]{2,0,1:T(8,128)} copy(f32[56,9,128]{2,1,0:T(8,128)} %shard_map.136) | data formatting | bytes 516096 | tf_op jit(solution)/shard_map/pallas_call | solution.py:352
Async XLA Ops:
  0.0 0.7 copy-start.4
  0.0 4.2 %copy-start.3 = (f32[3,9,9,128]{3,0,2,1:T(4,128)S(1)}, f32[3,9,9,128]{3,0,2,1:T(4,128)}, u32[]{:S(2)}) copy-start(f32[3,9,9,128]{3,0,2,1:T(4,128)} %param.15) | copy-start | bytes 373252
  4.3 1.0 %copy-start.1 = (f32[4,9,9,128]{3,0,2,1:T(4,128)S(1)}, f32[4,9,9,128]{3,0,2,1:T(4,128)}, u32[]{:S(2)}) copy-start(f32[4,9,9,128]{3,0,2,1:T(4,128)} %param.21) | copy-start | bytes 497668
  5.3 1.0 %copy-start.2 = (f32[4,9,9,128]{3,0,2,1:T(4,128)S(1)}, f32[4,9,9,128]{3,0,2,1:T(4,128)}, u32[]{:S(2)}) copy-start(f32[4,9,9,128]{3,0,2,1:T(4,128)} %param.22) | copy-start | bytes 497668
  6.2 1.1 %copy-start = (f32[56,9,128]{2,0,1:T(8,128)S(1)}, f32[56,9,128]{2,0,1:T(8,128)}, u32[]{:S(2)}) copy-start(f32[56,9,128]{2,0,1:T(8,128)} %param.14) | copy-start | bytes 774148

commit v2 on v1

v2 whole, which is shorter than its diff:
```python
import jax
import jax.numpy as jnp
from jax import lax
from jax.experimental import pallas as pl
from jax.experimental.pallas import tpu as pltpu
from jax.sharding import PartitionSpec as P

BASIS = 56
QUANTITIES = 9
FACE_BASIS = 21
DERIVATIVES = 6
SUBSTEPS = 4
LANES = 128
FACES = 4
DIRECTIONS = 6
FACE_ROWS = 24
CHUNKS = 3
CHUNK_ROWS = 64
BLOCKS = ((0, 4), (4, 8), (8, 9))
MESH = pl.DeviceIdType.MESH
AXES = ("gx", "gy", "gz")

f32 = jnp.float32
bf16 = jnp.bfloat16


def halves(value):
    high = value.astype(bf16).astype(f32)
    return high, value - high


def stacked(value):
    high, low = halves(value)
    return jnp.concatenate([high, low, high], axis=0).astype(bf16)


def place(rows, columns, offsets):
    row = lax.broadcasted_iota(jnp.int32, (rows, columns), 0)
    column = lax.broadcasted_iota(jnp.int32, (rows, columns), 1)
    hit = column == row + offsets[0]
    for offset in offsets[1:]:
        hit = hit | (column == row + offset)
    return jnp.where(hit, 1.0, 0.0).astype(bf16)


def widened(matrix, columns, first, second, third, turned=False):
    high, low = halves(matrix)
    depth = matrix.shape[0 if turned else 1]
    dims = (((0 if turned else 1,), (0,)), ((), ()))
    both = place(depth, columns, (first, second))
    return lax.dot_general(
        high.astype(bf16), both, dims, preferred_element_type=f32
    ) + lax.dot_general(
        low.astype(bf16), place(depth, columns, (third,)), dims, preferred_element_type=f32
    )


def dot(left, right):
    return jnp.dot(left, right, preferred_element_type=f32)


def kernel(
    sol_ref, jac_ref, ds_ref, vs_ref, fp_ref, fl_ref, fr_ref, ls_ref, ns_ref,
    cluster_ref, neigh_ref, orient_ref, faces_ref, counts_ref, out_ref,
    own, flux, integ, mixed_0, mixed_1, volume, projected, table, pair,
    inner, total, zface, jac_b, ls_b, ns_b, weights,
    d_mat, v_mat, p_mat, l_mat, r_mat, build, build2, send_hot, recv_hot,
    send_buf, recv_buf, send_sem, recv_sem,
):
    cur = out_ref
    mixed = (mixed_0, mixed_1)
    index = [lax.axis_index(name) for name in AXES]
    count = [lax.axis_size(name) for name in AXES]
    has_lower = [index[a] > 0 for a in range(3)]
    has_higher = [index[a] < count[a] - 1 for a in range(3)]

    barrier = pltpu.get_barrier_semaphore()
    arrivals = jnp.int32(0)
    for a in range(3):
        for there, step in ((has_lower[a], -1), (has_higher[a], 1)):
            arrivals = arrivals + there.astype(jnp.int32)

            @pl.when(there)
            def _(a=a, step=step):
                pl.semaphore_signal(
                    barrier, inc=1, device_id={AXES[a]: index[a] + step}, device_id_type=MESH
                )

    for d in range(3):
        for q in range(QUANTITIES):
            for p in range(QUANTITIES):
                jac_b[(d * 9 + q) * 9 + p] = jnp.broadcast_to(jac_ref[q, p, d : d + 1, :], (8, LANES))
    d_mat[...] = widened(-ds_ref[...].reshape(3 * BASIS, BASIS), 3 * BASIS, 0, BASIS, 2 * BASIS).astype(bf16)
    for q in range(QUANTITIES):
        cur[q] = sol_ref[q]
        own[q] = jnp.zeros((BASIS, LANES), f32)
        flux[q] = jnp.zeros((BASIS, LANES), f32)
    build[...] = jnp.zeros_like(build)
    for j in range(FACES):
        build[j * FACE_ROWS : j * FACE_ROWS + FACE_BASIS, :] = widened(
            fp_ref[:, j, :], 3 * BASIS, 0, BASIS, 2 * BASIS
        )
    p_mat[...] = build[...].astype(bf16)
    slot = lax.broadcasted_iota(jnp.int32, (1, LANES), 1)
    face_row = lax.broadcasted_iota(jnp.int32, (FACES * LANES, LANES), 0)
    for k in range(DIRECTIONS):
        named = jnp.where(slot < counts_ref[:, k : k + 1], faces_ref[k : k + 1, :], -1)
        send_hot[:, k * LANES : (k + 1) * LANES] = jnp.where(face_row == named, 1.0, 0.0).astype(bf16)
    for a in range(3):
        for side in range(2):

            @pl.when(jnp.logical_not((has_lower, has_higher)[side][a]))
            def _(k=2 * a + side):
                for step in range(SUBSTEPS):
                    recv_buf[step, k] = jnp.zeros((CHUNKS, CHUNK_ROWS, LANES), f32)

    def late_constants():
        for start, rows, value in ((0, 768, 0), (768, 256, 1024), (1024, 256, 768)):
            block_row = lax.broadcasted_iota(jnp.int32, (rows, LANES), 0) + value
            for i in range(FACES):
                recv_hot[start : start + rows, i * LANES : (i + 1) * LANES] = jnp.where(
                    block_row == neigh_ref[i : i + 1, :], 1.0, 0.0
                ).astype(bf16)
        for i in range(FACES):
            for q in range(QUANTITIES):
                for p in range(QUANTITIES):
                    at = (i * 9 + q) * 9 + p
                    ls_b[at] = jnp.broadcast_to(ls_ref[q, p, i : i + 1, :], (8, LANES))
                    ns_b[at] = jnp.broadcast_to(ns_ref[q, p, i : i + 1, :], (8, LANES))
        v_mat[...] = widened(vs_ref[...].reshape(3 * BASIS, BASIS), 3 * BASIS, 0, BASIS, 2 * BASIS).astype(bf16)
        width = FACES * FACE_ROWS
        joined = jnp.zeros((BASIS, 3 * width), f32)
        for i in range(FACES):
            at = i * FACE_ROWS
            joined = joined + widened(fl_ref[:, i, :], 3 * width, at, width + at, 2 * width + at, True)
        l_mat[...] = joined.astype(bf16)
        build2[...] = jnp.zeros_like(build2)
        for o in range(3):
            build2[o * FACE_ROWS : o * FACE_ROWS + FACE_BASIS, :] = widened(
                fr_ref[o], 3 * FACE_ROWS, 0, FACE_ROWS, 2 * FACE_ROWS
            )
        r_mat[...] = build2[...].astype(bf16)
        total[...] = jnp.zeros_like(total)

    def columns(q, width=1):
        return slice(q * LANES, (q + width) * LANES)

    def tall(value, scale):
        shape = value.shape
        return (value.reshape(shape[0] // 8, 8, LANES) * scale[None]).reshape(shape)

    def beside(pieces):
        return pieces[0] if len(pieces) == 1 else jnp.concatenate(pieces, axis=1)

    def mix(matrix, slot, first, pieces):
        for q in range(0, len(pieces), 2):
            some = pieces[q : q + 2]
            product = dot(matrix[...], beside(some))
            for w in range(len(some)):
                mixed[slot][first + q + w] = product[:, columns(w)]

    def apply_jacobians(slot, p0, wide):
        sums = [None] * wide
        for q in range(QUANTITIES):
            for d in range(3):
                part = mixed[slot][q, d * BASIS : (d + 1) * BASIS, :]
                for w in range(wide):
                    term = tall(part, jac_b[(d * 9 + q) * 9 + p0 + w])
                    sums[w] = term if sums[w] is None else sums[w] + term
        return sums

    def copy(s, k):
        a, side = k // 2, k % 2
        return pltpu.make_async_remote_copy(
            src_ref=send_buf.at[s, k],
            dst_ref=recv_buf.at[s, k],
            send_sem=send_sem.at[s, k],
            recv_sem=recv_sem.at[s, k],
            device_id={AXES[a]: index[a] + (1, -1)[side]},
            device_id_type=MESH,
        )

    def sends(k):
        return (has_higher, has_lower)[k % 2][k // 2]

    def receives(k):
        return (has_lower, has_higher)[k % 2][k // 2]

    def combined(product, chunk):
        at = 2 * CHUNK_ROWS * chunk
        return product[at : at + CHUNK_ROWS] + product[at + CHUNK_ROWS : at + 2 * CHUNK_ROWS]

    def fill_pair(chunk, column, value):
        high, low = halves(value)
        at = 2 * CHUNK_ROWS * chunk
        pair[at : at + CHUNK_ROWS, columns(column)] = high.astype(bf16)
        pair[at + CHUNK_ROWS : at + 2 * CHUNK_ROWS, columns(column)] = low.astype(bf16)

    period = jnp.left_shift(jnp.ones((8, LANES), jnp.int32), jnp.broadcast_to(cluster_ref[...], (8, LANES)))

    def substep(s, carry):
        offset = (s & (period - 1)).astype(f32)
        ending = ((s + 1) & (period - 1)) == 0
        upper, lower = (offset + 1.0) * 0.25, offset * 0.25
        up, low, factorial = upper, lower, 1.0
        for m in range(DERIVATIVES):
            factorial = factorial * (m + 1)
            weights[m] = (up - low) * (1.0 / factorial)
            up, low = up * upper, low * lower

        held = {}
        for first, last in BLOCKS:
            pieces = []
            for q in range(first, last):
                value = cur[q]
                pieces.append(stacked(value))
                held[q] = tall(value, weights[0])
            mix(d_mat, 0, first, pieces)
        for m in range(1, DERIVATIVES - 1):
            here, there = (m - 1) % 2, m % 2
            for first, last in BLOCKS:
                fresh = apply_jacobians(here, first, last - first)
                pieces = []
                for w, value in enumerate(fresh):
                    pieces.append(stacked(value))
                    held[first + w] = held[first + w] + tall(value, weights[m])
                mix(d_mat, there, first, pieces)
        here = (DERIVATIVES - 2) % 2
        for chunk in range(CHUNKS):
            first = 3 * chunk
            pieces = []
            fresh = apply_jacobians(here, first, 3)
            for w, value in enumerate(fresh):
                value = held[first + w] + tall(value, weights[DERIVATIVES - 1])
                integ[first + w] = value
                pieces.append(stacked(value))
            for q, width in ((0, 2), (2, 1)):
                product = dot(p_mat[...], beside(pieces[q : q + width]))
                for w in range(width):
                    at = q + w
                    projected[first + at] = product[:, columns(w)]
                    for j in range(FACES):
                        table[chunk, j, at * FACE_BASIS : at * FACE_BASIS + FACE_ROWS, :] = product[
                            j * FACE_ROWS : (j + 1) * FACE_ROWS, columns(w)
                        ]
            for j in range(FACES):
                fill_pair(chunk, j, table[chunk, j, 0:CHUNK_ROWS, :])

        @pl.when(s == 0)
        def _():
            pl.semaphore_wait(barrier, arrivals)

        for a in (1, 2, 0):
            product = dot(pair[:, 0 : FACES * LANES], send_hot[:, columns(2 * a, 2)])
            for chunk in range(CHUNKS):
                part = combined(product, chunk)
                for side in range(2):
                    send_buf[s, 2 * a + side, chunk] = part[:, columns(side)]
            for k in (2 * a, 2 * a + 1):

                @pl.when(sends(k))
                def _(k=k):
                    copy(s, k).start()

        @pl.when(s == 0)
        def _():
            late_constants()

        pieces = []
        for q in range(QUANTITIES):
            value = own[q] + integ[q]
            own[q] = value
            pieces.append(stacked(value))
        mix(v_mat, 0, 0, pieces)
        for first in range(0, QUANTITIES, 3):
            for w, value in enumerate(apply_jacobians(0, first, 3)):
                volume[first + w] = value
        for i in range(FACES):
            rows = slice(i * FACE_ROWS, (i + 1) * FACE_ROWS)
            for p0 in range(0, QUANTITIES, 3):
                sums = [None] * 3
                for q in range(QUANTITIES):
                    part = projected[q, rows, :]
                    for w in range(3):
                        term = tall(part, ls_b[(i * 9 + q) * 9 + p0 + w])
                        sums[w] = term if sums[w] is None else sums[w] + term
                for w in range(3):
                    zface[p0 + w, rows, :] = sums[w]

        for k in (4, 5, 0, 1):

            @pl.when(receives(k))
            def _(k=k):
                copy(s, k).wait_recv()

        for at, k in enumerate((0, 1, 4, 5)):
            for chunk in range(CHUNKS):
                fill_pair(chunk, FACES + at, recv_buf[s, k, chunk])
        early = 8 * LANES
        for i in range(0, FACES, 2):
            product = dot(pair[:, 0:early], recv_hot[0:early, columns(i, 2)])
            for chunk in range(CHUNKS):
                part = combined(product, chunk)
                for w in range(2):
                    inner[chunk, i + w] = part[:, columns(w)]

        for k in (2, 3):

            @pl.when(receives(k))
            def _(k=k):
                copy(s, k).wait_recv()

        for chunk in range(CHUNKS):
            for k in (2, 3):
                fill_pair(chunk, 6 + k, recv_buf[s, k, chunk])
        for i in range(0, FACES, 2):
            product = dot(pair[:, early:], recv_hot[early:, columns(i, 2)])
            for chunk in range(CHUNKS):
                part = combined(product, chunk)
                for w in range(2):
                    total[i + w, chunk, 0:CHUNK_ROWS, :] = inner[chunk, i + w] + part[:, columns(w)]
        for i in range(FACES):
            rows = slice(i * FACE_ROWS, (i + 1) * FACE_ROWS)
            turn = jnp.broadcast_to(orient_ref[i : i + 1, :], (8, LANES))[None]
            pieces = []
            for q in range(QUANTITIES):
                at = (q % 3) * FACE_BASIS
                pieces.append(stacked(total[i, q // 3, at : at + FACE_ROWS, :]))
            picked = []
            for q0 in range(0, QUANTITIES, 2):
                wide = min(2, QUANTITIES - q0)
                product = dot(r_mat[...], beside(pieces[q0 : q0 + wide]))
                for w in range(wide):
                    parts = [
                        product[o * FACE_ROWS : (o + 1) * FACE_ROWS, columns(w)].reshape(3, 8, LANES)
                        for o in range(3)
                    ]
                    value = jnp.where(turn == 0, parts[0], jnp.where(turn == 1, parts[1], parts[2]))
                    picked.append(value.reshape(FACE_ROWS, LANES))
            for p0 in range(0, QUANTITIES, 3):
                sums = [zface[p0 + w, rows, :] for w in range(3)]
                for q in range(QUANTITIES):
                    part = picked[q]
                    for w in range(3):
                        sums[w] = sums[w] + tall(part, ns_b[(i * 9 + q) * 9 + p0 + w])
                for w in range(3):
                    zface[p0 + w, rows, :] = sums[w]

        for p in range(0, QUANTITIES, 2):
            width = min(2, QUANTITIES - p)
            product = dot(l_mat[...], beside([stacked(zface[p + w]) for w in range(width)]))
            for w in range(width):
                at = p + w
                done = ending[None]
                fluxes = (flux[at] + product[:, columns(w)]).reshape(7, 8, LANES)
                old = cur[at].reshape(7, 8, LANES)
                fresh = old + volume[at].reshape(7, 8, LANES) - fluxes
                cur[at] = jnp.where(done, fresh, old).reshape(BASIS, LANES)
                flux[at] = jnp.where(done, 0.0, fluxes).reshape(BASIS, LANES)
                own[at] = jnp.where(done, 0.0, own[at].reshape(7, 8, LANES)).reshape(BASIS, LANES)
        return carry

    lax.fori_loop(0, SUBSTEPS, substep, 0)

    for s in range(SUBSTEPS):
        for k in range(DIRECTIONS):

            @pl.when(sends(k))
            def _(s=s, k=k):
                copy(s, k).wait_send()


def local(*arrays):
    arrays = list(arrays)
    arrays[0] = arrays[0].transpose(1, 0, 2)
    for at in (1, 7, 8):
        arrays[at] = arrays[at].transpose(1, 2, 0, 3)
    arrays[4] = arrays[4].transpose(1, 0, 2)
    arrays[5] = arrays[5].transpose(2, 0, 1)
    arrays[9] = arrays[9].reshape(1, LANES)
    arrays[13] = arrays[13].reshape(1, DIRECTIONS)
    state = pltpu.VMEM((QUANTITIES, BASIS, LANES), f32)
    vmem = pltpu.VMEM
    advanced = pl.pallas_call(
        kernel,
        out_shape=jax.ShapeDtypeStruct((QUANTITIES, BASIS, LANES), f32),
        in_specs=[pl.BlockSpec(memory_space=pltpu.VMEM)] * len(arrays),
        out_specs=pl.BlockSpec(memory_space=pltpu.VMEM),
        scratch_shapes=[
            state,
            state,
            state,
            vmem((QUANTITIES, 3 * BASIS, LANES), f32),
            vmem((QUANTITIES, 3 * BASIS, LANES), f32),
            state,
            vmem((QUANTITIES, FACES * FACE_ROWS, LANES), f32),
            vmem((CHUNKS, FACES, 72, LANES), f32),
            vmem((CHUNKS * 2 * CHUNK_ROWS, (FACES + DIRECTIONS) * LANES), bf16),
            vmem((CHUNKS, FACES, CHUNK_ROWS, LANES), f32),
            vmem((FACES, CHUNKS, 72, LANES), f32),
            vmem((QUANTITIES, FACES * FACE_ROWS, LANES), f32),
            vmem((3 * 81, 8, LANES), f32),
            vmem((4 * 81, 8, LANES), f32),
            vmem((4 * 81, 8, LANES), f32),
            vmem((DERIVATIVES, 8, LANES), f32),
            vmem((3 * BASIS, 3 * BASIS), bf16),
            vmem((3 * BASIS, 3 * BASIS), bf16),
            vmem((FACES * FACE_ROWS, 3 * BASIS), bf16),
            vmem((BASIS, 3 * FACES * FACE_ROWS), bf16),
            vmem((3 * FACE_ROWS, 3 * FACE_ROWS), bf16),
            vmem((FACES * FACE_ROWS, 3 * BASIS), f32),
            vmem((3 * FACE_ROWS, 3 * FACE_ROWS), f32),
            vmem((FACES * LANES, DIRECTIONS * LANES), bf16),
            vmem(((FACES + DIRECTIONS) * LANES, FACES * LANES), bf16),
            vmem((SUBSTEPS, DIRECTIONS, CHUNKS, CHUNK_ROWS, LANES), f32),
            vmem((SUBSTEPS, DIRECTIONS, CHUNKS, CHUNK_ROWS, LANES), f32),
            pltpu.SemaphoreType.DMA((SUBSTEPS, DIRECTIONS)),
            pltpu.SemaphoreType.DMA((SUBSTEPS, DIRECTIONS)),
        ],
        compiler_params=pltpu.CompilerParams(
            collective_id=0, has_side_effects=True, vmem_limit_bytes=56 * 1024 * 1024
        ),
    )(*arrays)
    return advanced.transpose(1, 0, 2)


def solution(mesh):
    spread = ("gx", "gy", "gz")
    return jax.shard_map(
        local,
        mesh=mesh,
        in_specs=(
            P(None, None, spread),
            P(None, None, None, spread),
            P(),
            P(),
            P(),
            P(),
            P(),
            P(None, None, None, spread),
            P(None, None, None, spread),
            P(spread),
            P(None, spread),
            P(None, spread),
            P(None, spread),
            P(None, spread),
        ),
        out_specs=P(None, None, spread),
        check_vma=False,
    )
```

time: 75.7 us -> 62.7 us (0.83)
  the two profiles are of different devices: /device:TPU:240 before, /device:TPU:126 now
where the time goes in v2:
time: 62.7 us; the launch traced here: 62.5 us
  Pallas kernels  60.9 us (97%)
  local copies, waits for them, and re-layouts  1.66 us (3%)
    pallas_call x1, Pallas kernels, local(): pl.pallas_call(kernel, out_shape=jax.ShapeDtypeStruct((QUANTITIES, BASIS,...  60.9 us
    unnamed x1, local copies, waits for them, and re-layouts  1.66 us

profile of v2, /device:TPU:126, one launch (start us, length us, event | category | flops | bytes accessed | tf_op | source)
XLA Modules:
  0.0 62.5 jit_solution(14643468041482899292)
XLA Ops:
  0.0 60.9 %shard_map.136 = f32[9,56,128]{2,1,0:T(8,128)} custom-call(f32[9,56,128]{2,1,0:T(8,128)} %bitcast.10, f32[9,9,3,128]{3,2,1,0:T(4,128)} %bitcast.11, f32[3,56,56]{2,1,0:T(8,128)} %ds_ref.1, f32[3,56,56]{2,1,0:T(8,128)} %vs_ref.1, f32[21,4,56]{2,1,0:T(4,128)} %bitcast.14, f32[21,4,56]{2,1,0:T(4,128)} %bitcast.15, f32[3,21,21]{2,1,0:T(8,128)} %fr_ref.1, ...), custom_call_target="tpu_custom_call" | custom-call | tf_op jit(solution)/shard_map/pallas_call | solution.py:384
  60.9 1.7 %copy.16 = f32[56,9,128]{2,0,1:T(8,128)} copy(f32[56,9,128]{2,0,1:T(8,128)} %bitcast.9) | data formatting | bytes 516096

commit v3 on v2

--- a/solution.py
+++ b/solution.py
@@ -60,14 +60,22 @@
 
 
 def kernel(
-    sol_ref, jac_ref, ds_ref, vs_ref, fp_ref, fl_ref, fr_ref, ls_ref, ns_ref,
+    sol_hbm, jac_hbm, ds_ref, vs_ref, fp_ref, fl_ref, fr_ref, ls_hbm, ns_hbm,
     cluster_ref, neigh_ref, orient_ref, faces_ref, counts_ref, out_ref,
     own, flux, integ, mixed_0, mixed_1, volume, projected, table, pair,
     inner, total, zface, jac_b, ls_b, ns_b, weights,
     d_mat, v_mat, p_mat, l_mat, r_mat, build, build2, send_hot, recv_hot,
-    send_buf, recv_buf, send_sem, recv_sem,
+    send_buf, recv_buf, send_sem, recv_sem, jac_ref, ls_ref, ns_ref, load_sem,
 ):
     cur = out_ref
+    loads = [
+        pltpu.make_async_copy(source, target, load_sem.at[at])
+        for at, (source, target) in enumerate(
+            ((jac_hbm, jac_ref), (sol_hbm, cur), (ls_hbm, ls_ref), (ns_hbm, ns_ref))
+        )
+    ]
+    for load in loads:
+        load.start()
     mixed = (mixed_0, mixed_1)
     index = [lax.axis_index(name) for name in AXES]
     count = [lax.axis_size(name) for name in AXES]
@@ -86,13 +94,13 @@
                     barrier, inc=1, device_id={AXES[a]: index[a] + step}, device_id_type=MESH
                 )
 
+    loads[0].wait()
     for d in range(3):
         for q in range(QUANTITIES):
             for p in range(QUANTITIES):
                 jac_b[(d * 9 + q) * 9 + p] = jnp.broadcast_to(jac_ref[q, p, d : d + 1, :], (8, LANES))
     d_mat[...] = widened(-ds_ref[...].reshape(3 * BASIS, BASIS), 3 * BASIS, 0, BASIS, 2 * BASIS).astype(bf16)
     for q in range(QUANTITIES):
-        cur[q] = sol_ref[q]
         own[q] = jnp.zeros((BASIS, LANES), f32)
         flux[q] = jnp.zeros((BASIS, LANES), f32)
     build[...] = jnp.zeros_like(build)
@@ -115,6 +123,8 @@
                     recv_buf[step, k] = jnp.zeros((CHUNKS, CHUNK_ROWS, LANES), f32)
 
     def late_constants():
+        loads[2].wait()
+        loads[3].wait()
         for start, rows, value in ((0, 768, 0), (768, 256, 1024), (1024, 256, 768)):
             block_row = lax.broadcasted_iota(jnp.int32, (rows, LANES), 0) + value
             for i in range(FACES):
@@ -197,6 +207,8 @@
         pair[at + CHUNK_ROWS : at + 2 * CHUNK_ROWS, columns(column)] = low.astype(bf16)
 
     period = jnp.left_shift(jnp.ones((8, LANES), jnp.int32), jnp.broadcast_to(cluster_ref[...], (8, LANES)))
+
+    loads[1].wait()
 
     def substep(s, carry):
         offset = (s & (period - 1)).astype(f32)
@@ -269,7 +281,7 @@
         pieces = []
         for q in range(QUANTITIES):
             value = own[q] + integ[q]
-            own[q] = value
+            own[q] = jnp.where(ending[None], 0.0, value.reshape(7, 8, LANES)).reshape(BASIS, LANES)
             pieces.append(stacked(value))
         mix(v_mat, 0, 0, pieces)
         for first in range(0, QUANTITIES, 3):
@@ -357,7 +369,6 @@
                 fresh = old + volume[at].reshape(7, 8, LANES) - fluxes
                 cur[at] = jnp.where(done, fresh, old).reshape(BASIS, LANES)
                 flux[at] = jnp.where(done, 0.0, fluxes).reshape(BASIS, LANES)
-                own[at] = jnp.where(done, 0.0, own[at].reshape(7, 8, LANES)).reshape(BASIS, LANES)
         return carry
 
     lax.fori_loop(0, SUBSTEPS, substep, 0)
@@ -384,7 +395,10 @@
     advanced = pl.pallas_call(
         kernel,
         out_shape=jax.ShapeDtypeStruct((QUANTITIES, BASIS, LANES), f32),
-        in_specs=[pl.BlockSpec(memory_space=pltpu.VMEM)] * len(arrays),
+        in_specs=[
+            pl.BlockSpec(memory_space=pl.ANY if at in (0, 1, 7, 8) else pltpu.VMEM)
+            for at in range(len(arrays))
+        ],
         out_specs=pl.BlockSpec(memory_space=pltpu.VMEM),
         scratch_shapes=[
             state,
@@ -416,6 +430,10 @@
             vmem((SUBSTEPS, DIRECTIONS, CHUNKS, CHUNK_ROWS, LANES), f32),
             pltpu.SemaphoreType.DMA((SUBSTEPS, DIRECTIONS)),
             pltpu.SemaphoreType.DMA((SUBSTEPS, DIRECTIONS)),
+            vmem((QUANTITIES, QUANTITIES, 3, LANES), f32),
+            vmem((QUANTITIES, QUANTITIES, FACES, LANES), f32),
+            vmem((QUANTITIES, QUANTITIES, FACES, LANES), f32),
+            pltpu.SemaphoreType.DMA((4,)),
         ],
         compiler_params=pltpu.CompilerParams(
             collective_id=0, has_side_effects=True, vmem_limit_bytes=56 * 1024 * 1024

time: 62.7 us -> 62.2 us (level)
  the two profiles are of different devices: /device:TPU:126 before, /device:TPU:240 now
where the time goes in v3:
time: 62.2 us; the launch traced here: 62 us
  Pallas kernels  60.3 us (97%)
  local copies, waits for them, and re-layouts  1.66 us (3%)
    pallas_call x1, Pallas kernels, local(): pl.pallas_call(kernel, out_shape=jax.ShapeDtypeStruct((QUANTITIES, BASIS,...  60.3 us
    unnamed x1, local copies, waits for them, and re-layouts  1.66 us

profile of v3, /device:TPU:240, one launch (start us, length us, event | category | flops | bytes accessed | tf_op | source)
XLA Modules:
  0.0 62.0 jit_solution(2052778776626015086)
XLA Ops:
  0.0 60.3 %shard_map.136 = f32[9,56,128]{2,1,0:T(8,128)} custom-call(f32[9,56,128]{2,1,0:T(8,128)} %bitcast.10, f32[9,9,3,128]{3,2,1,0:T(4,128)} %bitcast.11, f32[3,56,56]{2,1,0:T(8,128)} %ds_ref.1, f32[3,56,56]{2,1,0:T(8,128)} %vs_ref.1, f32[21,4,56]{2,1,0:T(4,128)} %bitcast.14, f32[21,4,56]{2,1,0:T(4,128)} %bitcast.15, f32[3,21,21]{2,1,0:T(8,128)} %fr_ref.1, ...), custom_call_target="tpu_custom_call" | custom-call | tf_op jit(solution)/shard_map/pallas_call | solution.py:395
  60.3 1.7 %copy.16 = f32[56,9,128]{2,0,1:T(8,128)} copy(f32[56,9,128]{2,0,1:T(8,128)} %bitcast.9) | data formatting | bytes 516096
